TPU v7x, 32 devices: a whole 2x2x4 slice. The times are simulated.
32 devices in a mesh: replica: 16 (over z, y, x), tensor: 2 (over core).
Axes of the slice: x: 2, y: 2, z: 4, core: 2. Of those that a mesh axis runs over, the one named last changes fastest.
Arguments:
- tokens: bfloat16 [8192, 8192], P(('replica', 'tensor')), may hold values from -6 to 6
- norm_gain: bfloat16 [8192], replicated, may hold values from 0.099609375 to 1.8984375
- key_weight: bfloat16 [16, 8192, 1024], P('replica', None, 'tensor'), may hold values from -0.0625 to 0.0625
- inner_params: bfloat16 [16, 2, 1024, 512], P('replica', 'tensor'), may hold values from -6 to 6
- outer_params: float32 [2, 1024, 512], P('tensor', 'replica'), may hold values from -6 to 6
- outer_momentum: float32 [2, 1024, 512], P('tensor', 'replica'), may hold values from -3 to 3
Outputs:
- key_rows: bfloat16 [8192, 1024], P('replica', 'tensor')
- new_outer: float32 [2, 1024, 512], P('tensor', 'replica')
- new_momentum: float32 [2, 1024, 512], P('tensor', 'replica')
- synced_params: bfloat16 [2, 1024, 512], P('tensor')
All inputs are finite; a program needn't handle non-finite values.
Results may differ from a plain program's by a relative error of at most 0.0049.
Values may be sent and summed in bfloat16 or wider, within the bound.
A program may use at most 64 MiB of HBM per device.

v0:
```python
import math

import jax
import jax.numpy as jnp
from jax import lax
from jax.sharding import PartitionSpec as P

HD = 128


EPSILON = 1e-05
ROPE_BASE = 500000.0
LR_OUTER = 0.7
MOMENTUM_OUTER = 0.9


def rotate(keys_f32, positions):
    rows = keys_f32.shape[0]
    cols = keys_f32.shape[1]
    half = HD // 2
    shaped = keys_f32.reshape(rows, cols // HD, HD)
    index = jnp.arange(half).astype(jnp.float32)
    inverse = jnp.exp(-(2.0 * index / HD) * math.log(ROPE_BASE))
    angles = positions[:, None] * inverse[None, :]
    cosine = jnp.cos(angles)[:, None, :]
    sine = jnp.sin(angles)[:, None, :]
    first = shaped[:, :, :half]
    second = shaped[:, :, half:]
    joined = jnp.concatenate(
        [first * cosine - second * sine, second * cosine + first * sine], axis=-1
    )
    return joined.reshape(rows, cols)


def forward_keys(tokens, norm_gain, key_weight):
    block_f32 = tokens.astype(jnp.float32)
    scale = lax.rsqrt(jnp.mean(block_f32 * block_f32, axis=-1, keepdims=True) + EPSILON)
    normed = (block_f32 * scale * norm_gain.astype(jnp.float32)).astype(jnp.bfloat16)
    weight = key_weight[0]
    piece = lax.all_gather(normed, "tensor", axis=0, tiled=True)
    projected = jnp.dot(piece, weight, preferred_element_type=jnp.float32)
    positions = jnp.arange(piece.shape[0], dtype=jnp.int32).astype(jnp.float32)
    return rotate(projected, positions).astype(jnp.bfloat16)


def nesterov(outer_rows, moment_rows, summed, replicas):
    delta = outer_rows - summed / replicas
    moment_next = MOMENTUM_OUTER * moment_rows + delta
    outer_next = outer_rows - LR_OUTER * (delta + MOMENTUM_OUTER * moment_next)
    return (outer_next, moment_next)


def owned_sum(local_params):
    return lax.psum_scatter(
        local_params.astype(jnp.float32), "replica", scatter_dimension=0, tiled=True
    )


def sync_fragment(inner_params, outer_params, outer_momentum):
    replicas = lax.axis_size("replica")
    local_params = inner_params[0, 0]
    summed = owned_sum(local_params)
    outer_next, moment_next = nesterov(outer_params[0], outer_momentum[0], summed, replicas)
    synced = lax.all_gather(outer_next.astype(jnp.bfloat16), "replica", axis=0, tiled=True)
    return (outer_next[None], moment_next[None], synced[None])


def body(tokens, norm_gain, key_weight, inner_params, outer_params, outer_momentum):
    key_rows = forward_keys(tokens, norm_gain, key_weight)
    new_outer, new_momentum, synced_params = sync_fragment(
        inner_params, outer_params, outer_momentum
    )
    return (key_rows, new_outer, new_momentum, synced_params)


def solution(mesh):
    in_specs = (
        P(("replica", "tensor"), None),
        P(),
        P("replica", None, "tensor"),
        P("replica", "tensor", None, None),
        P("tensor", "replica", None),
        P("tensor", "replica", None),
    )
    out_specs = (
        P("replica", "tensor"),
        P("tensor", "replica", None),
        P("tensor", "replica", None),
        P("tensor", None, None),
    )
    return jax.shard_map(body, mesh=mesh, in_specs=in_specs, out_specs=out_specs, check_vma=False)
```

profile of v0, /device:TPU:0, one launch (start us, length us, event | category | flops | bytes accessed | tf_op | source)
XLA Modules:
  0.0 188.0 jit_solution(16721491939471057100)
XLA Ops:
  7.2 0.0 copy-start.1
  7.2 0.0 copy-start.2
  7.2 0.0 reduce-scatter.2.cloned.1.call-start
  7.2 2.9 %bitcast_convert_fusion = f32[1024,512]{1,0:T(8,128)} fusion(bf16[1,1,1024,512]{3,2,1,0:T(8,128)(2,1)} %param.9), kind=kLoop, calls=%fused_computation.7 | loop fusion | flops 524288 | bytes 3145728 | tf_op jit(solution)/shard_map/convert_element_type | solution.py:55
  10.1 0.0 reduce-scatter.2.cloned.1.call-update
  10.2 0.0 all-gather.5.cloned.1.call-start
  10.2 0.7 convert_element_type.49
  10.9 3.1 %fusion = f32[256]{0:T(256)S(1)} fusion(bf16[256,8192]{1,0:T(8,128)(2,1)} %param.6), kind=kLoop, calls=%fused_computation.2 | loop fusion | flops 6291200 | bytes 4195328 | tf_op jit(solution)/shard_map/reduce_sum | solution.py:37
  14.1 79.6 %reduce-scatter.2.cloned.1.call-done = f32[64,512]{1,0:T(8,128)} async-done(((f32[1024,512]{1,0:T(8,128)}), f32[64,512]{1,0:T(8,128)}) %reduce-scatter.2.cloned.1.call-update) | async-done | bytes 131088 | tf_op jit(solution)/shard_map/reduce_scatter | solution.py:54
  93.6 0.0 copy-done.1
  93.6 0.0 copy-done.2
  93.7 1.7 fusion.6
  95.3 0.0 all-gather.5.cloned.1.call-update
  95.3 0.0 all-gather.3.cloned.1.call-start
  95.4 5.3 %fusion.2 = bf16[256,8192]{1,0:T(8,128)(2,1)} fusion(bf16[256,8192]{1,0:T(8,128)(2,1)} %param.6, f32[8192]{0:T(1024)S(1)} %convert_element_type.49, f32[256]{0:T(256)S(1)} %add_rsqrt_fusion), kind=kLoop, calls=%fused_computation.4 | loop fusion | flops 8388608 | bytes 8422400 | tf_op jit(solution)/shard_map/convert_element_type | solution.py:38
  100.7 0.0 all-gather.3.cloned.1.call-update
  100.7 12.1 %copy.12 = bf16[512,8192]{1,0:T(8,128)(2,1)} copy(bf16[512,8192]{0,1:T(8,128)(2,1)} %bitcast.42) | data formatting | bytes 16777216 | tf_op jit(solution)/shard_map/dot_general | solution.py:41
  112.8 0.5 multiply_cosine_fusion
  113.3 36.2 %all-gather.5.cloned.1.call-done = bf16[1024,512]{1,0:T(8,128)(2,1)} async-done(((bf16[64,512]{1,0:T(8,128)(2,1)}), bf16[1024,512]{1,0:T(8,128)(2,1)}) %all-gather.5.cloned.1.call-update) | async-done | bytes 1048592 | tf_op jit(solution)/shard_map/all_gather | solution.py:64
  149.5 20.2 %all-gather.3.cloned.1.call-done = bf16[512,8192]{1,0:T(8,128)(2,1)} async-done(((bf16[256,8192]{1,0:T(8,128)(2,1)}), bf16[512,8192]{1,0:T(8,128)(2,1)}) %all-gather.3.cloned.1.call-update) | async-done | bytes 8388624 | tf_op jit(solution)/shard_map/all_gather | solution.py:40
  169.8 0.0 copy-start
  169.8 9.5 %fusion.3 = f32[512,4,128]{0,2,1:T(8,128)S(1)} fusion(bf16[4,128,8192]{2,1,0:T(8,128)(2,1)} %bitcast.43, bf16[512,8192]{1,0:T(8,128)(2,1)} %all-gather.3.cloned.1.call-done), kind=kOutput, calls=%fused_computation.5 | convolution fusion | flops 4294967296 | bytes 17825792 | tf_op jit(solution)/shard_map/dot_general | solution.py:41
  179.3 0.2 subtract_convert_fusion
  179.5 1.0 copy.11
  180.5 0.0 copy-done
  180.5 1.0 copy.14
  (4 shorter events, 0.1 us)
Async XLA Ops:
  7.2 86.5 %copy-start.1 = (f32[1,64,512]{2,1,0:T(8,128)S(1)}, f32[1,64,512]{2,1,0:T(8,128)}, u32[]{:S(2)}) copy-start(f32[1,64,512]{2,1,0:T(8,128)} %param.11) | copy-start | bytes 393220
  7.2 86.5 %copy-start.2 = (f32[1,64,512]{2,1,0:T(8,128)S(1)}, f32[1,64,512]{2,1,0:T(8,128)}, u32[]{:S(2)}) copy-start(f32[1,64,512]{2,1,0:T(8,128)} %param.10) | copy-start | bytes 393220
  7.2 86.5 %reduce-scatter.2.cloned.1.call-start = ((), (), s32[]{:S(2)}) async-start(), calls=%async_computation.2 | async-start | bytes 2228224 | tf_op jit(solution)/shard_map/reduce_scatter | solution.py:54
  10.2 139.4 %all-gather.5.cloned.1.call-start = ((), (), s32[]{:S(2)}) async-start(), calls=%async_computation.3 | async-start | bytes 1114112 | tf_op jit(solution)/shard_map/all_gather | solution.py:64
  95.3 74.4 %all-gather.3.cloned.1.call-start = ((), (), s32[]{:S(2)}) async-start(), calls=%async_computation.1 | async-start | bytes 12582912 | tf_op jit(solution)/shard_map/all_gather | solution.py:40
  169.8 10.8 %copy-start = (bf16[1024,512]{1,0:T(8,128)(2,1)S(1)}, bf16[1024,512]{1,0:T(8,128)(2,1)}, u32[]{:S(2)}) copy-start(bf16[1024,512]{1,0:T(8,128)(2,1)} %all-gather.5.cloned.1.call-done) | copy-start | bytes 3145732
Sparse Core Ops, SparseCore 0:
  10.3 83.3 reduce-scatter.1
  97.0 52.5 all-gather.4
  151.1 18.6 all-gather.2
where the time goes:
time: 189 us; the launch traced here: 188 us
  waiting for transfers between devices  136 us (72%)
  other arithmetic  14.5 us (8%)
  local copies, waits for them, and re-layouts  14.1 us (7%)
  between operations  13.8 us (7%)
  matrix products  9.51 us (5%)
    reduce_scatter x1, waiting for transfers between devices, owned_sum(): lax.psum_scatter(local_params.astype(jnp.float32), 'replica', scatter_dim...  79.6 us
    all_gather x1, waiting for transfers between devices, sync_fragment(): lax.all_gather(outer_next.astype(jnp.bfloat16), 'replica', axis=0, tiled=...  36.2 us
    all_gather x1, waiting for transfers between devices, forward_keys(): piece = lax.all_gather(normed, 'tensor', axis=0, tiled=True)  20.2 us
    dot_general x1, local copies, waits for them, and re-layouts, forward_keys(): projected = jnp.dot(piece, weight, preferred_element_type=jnp.float32)  12.1 us
    dot_general x1, matrix products, forward_keys(): projected = jnp.dot(piece, weight, preferred_element_type=jnp.float32)  9.51 us
    convert_element_type x1, other arithmetic, forward_keys(): (block_f32 * scale * norm_gain.astype(jnp.float32)).astype(jnp.bfloat16)  5.3 us
  transfers between devices with their start and end apart: 3, of which 3 were waited for; matrix products, arithmetic and copies ran while one was open for 12% of the time, Pallas kernels for 0%

commit v1 on v0

v1 whole, which is shorter than its diff:
```python
import functools
import math

import jax
import jax.numpy as jnp
import numpy as np
from jax import lax
from jax.experimental import pallas as pl
from jax.experimental.pallas import tpu as pltpu
from jax.sharding import PartitionSpec as P

HD = 128
EPSILON = 1e-05
ROPE_BASE = 500000.0
LR_OUTER = 0.7
MOMENTUM_OUTER = 0.9

MESH = pl.DeviceIdType.MESH
F32 = jnp.float32
BF16 = jnp.bfloat16

NORM_ROWS = 32
NORM_COLS = 512
K_STEP = 1024


def rotary_tables(rows):
    half = HD // 2
    index = np.arange(half, dtype=np.float32)
    inverse = np.exp(-(2.0 * index / HD) * math.log(ROPE_BASE)).astype(np.float32)
    angles = (np.arange(rows, dtype=np.float32)[:, None] * inverse[None, :]).astype(np.float64)
    cosine, sine = np.cos(angles), np.sin(angles)
    return np.stack(
        [np.concatenate([cosine, cosine], 1), np.concatenate([-sine, sine], 1)]
    ).astype(np.float32)


def kernel(
    sizes,
    tokens, gain, weight, inner, outer, moment, tables,
    keys_out, outer_out, moment_out, synced,
    tok_v, gain_v, w_v, inner_v, outer_v, moment_v, tables_v, normed_v, acc_v, keys_v,
    rs1a, rs1b, part1a, part1b, keepa, keepb, rs2a, rs2b, part2, own, rs3, piece_v,
    load_sem, tok_sem, w_sem, store_sem,
    s1_send, s1_recv, s2_send, s2_recv, s3_send, s3_recv,
    gz_send, gz_recv, gx_send, gx_recv, gy_send, gy_recv, dx_send, dx_recv, dy_send, dy_recv,
    n_send, n_recv,
):
    Z, T, tr, D, nc, rp, FC, nch, nw = sizes
    H = FC // 2
    R = Z * 4
    rep = lax.axis_index("replica")
    me_t = lax.axis_index("tensor")
    z, y, x = rep // 4, lax.rem(rep // 2, 2), lax.rem(rep, 2)
    oy, ox = 1 - y, 1 - x
    x_peer = (z * 4 + y * 2 + ox, me_t)
    y_peer = (z * 4 + oy * 2 + x, me_t)
    offsets = sorted(range(1, Z), key=lambda o: (-min(o, Z - o), o)) + [0]
    last = Z - 1

    def z_at(o):
        return lax.rem(z + o, Z)

    def z_peer(o):
        return (z_at(o) * 4 + y * 2 + x, me_t)

    rows_per = tr // nch
    k_per = D // nw
    load_inner = pltpu.make_async_copy(inner, inner_v, load_sem.at[0])
    load_gain = pltpu.make_async_copy(gain, gain_v, load_sem.at[1])
    load_outer = pltpu.make_async_copy(outer, outer_v, load_sem.at[2])
    load_moment = pltpu.make_async_copy(moment, moment_v, load_sem.at[3])
    load_tables = pltpu.make_async_copy(tables, tables_v, load_sem.at[4])
    load_tok = [
        pltpu.make_async_copy(
            tokens.at[pl.ds(c * rows_per, rows_per)],
            tok_v.at[pl.ds(c * rows_per, rows_per)],
            tok_sem.at[c],
        )
        for c in range(nch)
    ]
    load_w = [
        pltpu.make_async_copy(
            weight.at[0, pl.ds(c * k_per, k_per)], w_v.at[pl.ds(c * k_per, k_per)], w_sem.at[c]
        )
        for c in range(nw)
    ]
    load_gain.start()
    load_tok[0].start()
    load_inner.start()
    for c in range(1, nch):
        load_tok[c].start()
    for c in range(nw):
        load_w[c].start()
    load_outer.start()
    load_moment.start()
    load_tables.start()

    barrier = pltpu.get_barrier_semaphore()
    partners = [x_peer, y_peer]
    partners += [z_peer(o) for o in range(1, Z)]
    partners += [(rep, lax.rem(me_t + k, T)) for k in range(1, T)]
    for partner in partners:
        pl.semaphore_signal(barrier, inc=1, device_id=partner, device_id_type=MESH)
    pl.semaphore_wait(barrier, len(partners))

    sent = []

    def remote(src, dst, send_sem, recv_sem, device):
        return pltpu.make_async_remote_copy(
            src_ref=src, dst_ref=dst, send_sem=send_sem, recv_sem=recv_sem,
            device_id=device, device_id_type=MESH,
        )

    def start(copy):
        copy.start()
        sent.append(copy)
        return copy

    first_a, first_b = [], []
    for d, o in enumerate(offsets):
        zc = z_at(o)
        first_a.append(start(remote(
            inner.at[zc, :, ox, :, pl.ds(0, H)], rs1a.at[d],
            s1_send.at[2 * d], s1_recv.at[2 * d], x_peer)))
        first_b.append(start(remote(
            inner.at[zc, oy, :, :, pl.ds(H, H)], rs1b.at[d],
            s1_send.at[2 * d + 1], s1_recv.at[2 * d + 1], y_peer)))

    def norm_copy(k, c, source, device):
        rows = pl.ds(c * rows_per, rows_per)
        i = (k - 1) * nch + c
        return remote(
            normed_v.at[source, rows], normed_v.at[source, rows], n_send.at[i], n_recv.at[i], device
        )

    def norm(c):
        if c == 0:
            load_gain.wait()
        load_tok[c].wait()

        def block(i, carry):
            rows = pl.ds(pl.multiple_of(c * rows_per + i * NORM_ROWS, NORM_ROWS), NORM_ROWS)
            total = jnp.zeros((NORM_ROWS, 128), F32)
            for j in range(0, D, 128):
                v = tok_v[rows, pl.ds(j, 128)].astype(F32)
                total = total + v * v
            scale = lax.rsqrt(jnp.sum(total, axis=-1, keepdims=True) / D + EPSILON)
            for j in range(0, D, NORM_COLS):
                cols = pl.ds(j, NORM_COLS)
                v = tok_v[rows, cols].astype(F32)
                normed_v[me_t, rows, cols] = (v * scale * gain_v[:, cols].astype(F32)).astype(BF16)
            return carry

        lax.fori_loop(0, rows_per // NORM_ROWS, block, 0)
        for k in range(1, T):
            start(norm_copy(k, c, me_t, (rep, lax.rem(me_t + k, T))))

    second_a, second_b, third = [None] * Z, [None] * Z, [None] * Z

    def step_a(d):
        zc = z_at(offsets[d])
        if d == 0:
            load_inner.wait()
        first_a[d].wait_recv()
        part1a[d] = (inner_v[zc, oy, x, :, :H].astype(F32) + rs1a[d, oy].astype(F32)).astype(BF16)
        second_a[d] = start(remote(
            part1a.at[d], rs2a.at[d], s2_send.at[2 * d], s2_recv.at[2 * d], y_peer))
        keepa[d] = inner_v[zc, y, x, :, :H].astype(F32) + rs1a[d, y].astype(F32)
        first_b[d].wait_recv()
        part1b[d] = (inner_v[zc, y, ox, :, H:].astype(F32) + rs1b[d, ox].astype(F32)).astype(BF16)
        second_b[d] = start(remote(
            part1b.at[d], rs2b.at[d], s2_send.at[2 * d + 1], s2_recv.at[2 * d + 1], x_peer))
        keepb[d] = inner_v[zc, y, x, :, H:].astype(F32) + rs1b[d, x].astype(F32)

    def step_b(d):
        second_a[d].wait_recv()
        second_b[d].wait_recv()
        suma = keepa[d] + rs2a[d].astype(F32)
        sumb = keepb[d] + rs2b[d].astype(F32)
        if d == last:
            own[:, :H] = suma
            own[:, H:] = sumb
        else:
            part2[d, :, :H] = suma.astype(BF16)
            part2[d, :, H:] = sumb.astype(BF16)
            third[d] = start(remote(
                part2.at[d], rs3.at[d], s3_send.at[d], s3_recv.at[d], z_peer(offsets[d])))

    stores = []

    def store(src, dst, i):
        copy = pltpu.make_async_copy(src, dst, store_sem.at[i])
        copy.start()
        stores.append(copy)

    here = synced.at[z, y, x]
    gather_z, gather_x, gather_y, diag_x, diag_y = ([None] * Z for _ in range(5))

    def spread(d, src):
        zp = lax.rem(z + Z - offsets[d], Z)
        dst = synced.at[zp, y, x]
        gather_y[d] = start(remote(src, dst, gy_send.at[d], gy_recv.at[d], y_peer))
        gather_x[d] = start(remote(src, dst, gx_send.at[d], gx_recv.at[d], x_peer))

    def step_c():
        load_outer.wait()
        load_moment.wait()
        summed = own[...]
        for d in range(last):
            third[d].wait_recv()
            summed = summed + rs3[d].astype(F32)
        outer_rows = outer_v[0]
        delta = outer_rows - summed / R
        moment_next = MOMENTUM_OUTER * moment_v[0] + delta
        outer_next = outer_rows - LR_OUTER * (delta + MOMENTUM_OUTER * moment_next)
        piece_v[...] = outer_next.astype(BF16)
        for d in range(last):
            gather_z[d] = start(remote(
                piece_v, here, gz_send.at[d], gz_recv.at[d], z_peer(offsets[d])))
        spread(last, piece_v)
        outer_v[0] = outer_next
        moment_v[0] = moment_next
        store(outer_v, outer_out, 0)
        store(moment_v, moment_out, 1)
        store(piece_v, here, 2)

    def step_z(d):
        zp = lax.rem(z + Z - offsets[d], Z)
        gather_z[d].wait_recv()
        spread(d, synced.at[zp, y, x])

    def step_f(d):
        zp = lax.rem(z + Z - offsets[d], Z)
        gather_y[d].wait_recv()
        from_y = synced.at[zp, oy, x, :, pl.ds(0, H)]
        diag_x[d] = start(remote(from_y, from_y, dx_send.at[d], dx_recv.at[d], x_peer))
        gather_x[d].wait_recv()
        from_x = synced.at[zp, y, ox, :, pl.ds(H, H)]
        diag_y[d] = start(remote(from_x, from_x, dy_send.at[d], dy_recv.at[d], y_peer))

    def project(k, part):
        slot = lax.rem(me_t + T - k, T)
        if k == 0:
            load_w[part].wait()
        elif part == 0:
            for c in range(nch):
                norm_copy(k, c, slot, (rep, lax.rem(me_t + k, T))).wait_recv()

        def block(i, carry):
            depth = pl.ds(pl.multiple_of(part * k_per + i * K_STEP, K_STEP), K_STEP)
            acc_v[...] += jnp.dot(
                normed_v[slot, :, depth], w_v[depth, :], preferred_element_type=F32
            )
            return carry

        if part == 0:
            acc_v[...] = jnp.zeros_like(acc_v)
        lax.fori_loop(0, k_per // K_STEP, block, 0)

    def turn(k):
        slot = lax.rem(me_t + T - k, T)
        if k == 0:
            load_tables.wait()
        rows = pl.ds(pl.multiple_of(slot * tr, tr), tr)
        cosine = tables_v[0, rows]
        sine = tables_v[1, rows]
        for h in range(nc // HD):
            cols = pl.ds(h * HD, HD)
            v = acc_v[:, cols]
            keys_v[rows, cols] = (v * cosine + pltpu.roll(v, HD // 2, 1) * sine).astype(BF16)
        store(keys_v.at[rows], keys_out.at[rows], 3 + k)

    compute = [functools.partial(norm, c) for c in range(nch)]
    for k in range(T):
        compute += [functools.partial(project, k, part) for part in range(nw)]
        compute.append(functools.partial(turn, k))
    compute = compute[::-1]

    def work(count=1):
        for _ in range(count):
            if compute:
                compute.pop()()

    work(1)
    for d in range(Z):
        work(1)
        step_a(d)
        if d >= 1:
            step_b(d - 1)
    work(1)
    step_b(last)
    work(max(3, len(compute) - 5))
    step_c()
    work(1)
    step_f(last)
    for d in range(last):
        work(1)
        step_z(d)
        if d >= 1:
            step_f(d - 1)
    work(len(compute))
    step_f(last - 1)
    for d in range(Z):
        diag_x[d].wait_recv()
        diag_y[d].wait_recv()
    for copy in sent:
        copy.wait_send()
    for copy in stores:
        copy.wait()


def solution(mesh):
    R, T = mesh.shape["replica"], mesh.shape["tensor"]
    Z = R // 4

    def body(tokens, norm_gain, key_weight, inner_params, outer_params, outer_momentum):
        tr, D = tokens.shape
        nc = key_weight.shape[2]
        rows, FC = inner_params.shape[2:]
        rp = rows // R
        H = FC // 2
        tok = tr * T
        nch = max(1, tr // 64)
        nw = 4
        inner = inner_params.reshape(Z, 2, 2, rp, FC)
        gain = norm_gain.reshape(1, D)
        tables = jnp.asarray(rotary_tables(tok))
        sizes = (Z, T, tr, D, nc, rp, FC, nch, nw)
        vm = pltpu.VMEM
        dma = lambda n: pltpu.SemaphoreType.DMA((n,))
        scratch = [
            vm((tr, D), BF16), vm((1, D), BF16), vm((D, nc), BF16),
            vm((Z, 2, 2, rp, FC), BF16), vm((1, rp, FC), F32), vm((1, rp, FC), F32),
            vm((2, tok, HD), F32), vm((T, tr, D), BF16), vm((tr, nc), F32), vm((tok, nc), BF16),
            vm((Z, 2, rp, H), BF16), vm((Z, 2, rp, H), BF16),
            vm((Z, rp, H), BF16), vm((Z, rp, H), BF16),
            vm((Z, rp, H), F32), vm((Z, rp, H), F32),
            vm((Z, rp, H), BF16), vm((Z, rp, H), BF16),
            vm((Z, rp, FC), BF16), vm((rp, FC), F32), vm((Z, rp, FC), BF16), vm((rp, FC), BF16),
            dma(5), dma(nch), dma(nw), dma(3 + T),
            dma(2 * Z), dma(2 * Z), dma(2 * Z), dma(2 * Z), dma(Z), dma(Z),
            dma(Z), dma(Z), dma(Z), dma(Z), dma(Z), dma(Z), dma(Z), dma(Z), dma(Z), dma(Z),
            dma(nch * (T - 1)), dma(nch * (T - 1)),
        ]
        anywhere = pl.BlockSpec(memory_space=pl.ANY)
        keys, outer_next, moment_next, synced = pl.pallas_call(
            functools.partial(kernel, sizes),
            out_shape=(
                jax.ShapeDtypeStruct((tok, nc), BF16),
                jax.ShapeDtypeStruct((1, rp, FC), F32),
                jax.ShapeDtypeStruct((1, rp, FC), F32),
                jax.ShapeDtypeStruct((Z, 2, 2, rp, FC), BF16),
            ),
            in_specs=[anywhere] * 7,
            out_specs=(anywhere,) * 4,
            scratch_shapes=scratch,
            compiler_params=pltpu.CompilerParams(
                collective_id=0, has_side_effects=True, vmem_limit_bytes=48 * 2**20
            ),
            name="outer_step_and_keys",
        )(tokens, gain, key_weight, inner, outer_params, outer_momentum, tables)
        return keys, outer_next, moment_next, synced.reshape(1, rows, FC)

    in_specs = (
        P(("replica", "tensor"), None),
        P(),
        P("replica", None, "tensor"),
        P("replica", "tensor", None, None),
        P("tensor", "replica", None),
        P("tensor", "replica", None),
    )
    out_specs = (
        P("replica", "tensor"),
        P("tensor", "replica", None),
        P("tensor", "replica", None),
        P("tensor", None, None),
    )
    return jax.shard_map(body, mesh=mesh, in_specs=in_specs, out_specs=out_specs, check_vma=False)
```

time: 189 us -> 46.5 us (0.25)
  waiting for transfers between devices: 136 us -> 0 us
  Pallas kernels: 0 us -> 37.7 us
  other arithmetic: 14.5 us -> 0 us
  between operations: 13.8 us -> 0.65 us
  matrix products: 9.51 us -> 0 us
  local copies, waits for them, and re-layouts: 14.1 us -> 7.88 us
    reduce_scatter x1 -> x0, waiting for transfers between devices: 79.6 us -> none  [owned_sum(): lax.psum_scatter(local_params.astype(jnp.float32), 'replica', scatter_dim...]
    all_gather x2 -> x0, waiting for transfers between devices: 56.4 us -> none  [the longest x1 36.2 us: sync_fragment(): lax.all_gather(outer_next.astype(jnp.bfloat16), 'replica', axis=0, tiled=...]
    pallas_call x0 -> x1, Pallas kernels: none -> 37.7 us  [body(): pl.pallas_call(functools.partial(kernel, sizes), out_shape=(jax.ShapeDtyp...]
    dot_general x1 -> x0, local copies, waits for them, and re-layouts: 12.1 us -> none  [forward_keys(): projected = jnp.dot(piece, weight, preferred_element_type=jnp.float32)]
    convert_element_type x5 -> x0, other arithmetic: 10.6 us -> none  [the longest x1 5.3 us: forward_keys(): (block_f32 * scale * norm_gain.astype(jnp.float32)).astype(jnp.bfloat16)]
    dot_general x1 -> x0, matrix products: 9.51 us -> none  [forward_keys(): projected = jnp.dot(piece, weight, preferred_element_type=jnp.float32)]
    unnamed x8 -> x12, local copies, waits for them, and re-layouts: 1.99 us -> 7.14 us
    reduce_sum x1 -> x0, other arithmetic: 3.1 us -> none  [forward_keys(): jnp.mean(block_f32 * block_f32, axis=-1, keepdims=True) + EPSILON]
  transfers between devices with their start and end apart: 3 -> 0, of which waited for: 3 -> 0; matrix products, arithmetic and copies ran while one was open for 12% -> 0% of each run, Pallas kernels for 0% -> 0%
where the time goes in v1:
time: 46.5 us; the launch traced here: 46.2 us
  Pallas kernels  37.7 us (81%)
  local copies, waits for them, and re-layouts  7.88 us (17%)
  between operations  0.65 us (1%)
    pallas_call x1, Pallas kernels, body(): pl.pallas_call(functools.partial(kernel, sizes), out_shape=(jax.ShapeDtyp...  37.7 us
    unnamed x12, local copies, waits for them, and re-layouts  7.14 us

profile of v1, /device:TPU:0, one launch (start us, length us, event | category | flops | bytes accessed | tf_op | source)
XLA Modules:
  0.0 46.2 jit_solution(282579463103078783)
XLA Ops:
  0.6 0.7 %reshape.17.gain = bf16[1,8192]{1,0:T(2,128)(2,1)S(1)} reshape(bf16[8192]{0:T(1024)(128)(2,1)} %param.8) | data formatting | bytes 32768 | tf_op jit(solution)/shard_map/reshape | solution.py:327
  1.4 0.0 copy-start
  1.4 1.2 %copy-done = bf16[1,1,1024,512]{3,2,1,0:T(8,128)(2,1)S(1)} copy-done((bf16[1,1,1024,512]{3,2,1,0:T(8,128)(2,1)S(1)}, bf16[1,1,1024,512]{3,2,1,0:T(8,128)(2,1)}, u32[]{:S(2)}) %copy-start) | copy-done | bytes 1048600
  2.6 0.0 copy-start.1
  2.6 1.0 %copy-done.1 = f32[2,512,128]{2,1,0:T(8,128)S(1)} copy-done((f32[2,512,128]{2,1,0:T(8,128)S(1)}, f32[2,512,128]{2,1,0:T(8,128)}, u32[]{:S(2)}) %copy-start.1) | copy-done | bytes 524312
  3.6 0.0 copy-start.2
  3.6 0.9 %copy-done.2 = f32[1,64,512]{2,1,0:T(8,128)S(1)} copy-done((f32[1,64,512]{2,1,0:T(8,128)S(1)}, f32[1,64,512]{2,1,0:T(8,128)}, u32[]{:S(2)}) %copy-start.2) | copy-done | bytes 131096
  4.5 0.0 copy-start.3
  4.5 0.9 %copy-done.3 = f32[1,64,512]{2,1,0:T(8,128)S(1)} copy-done((f32[1,64,512]{2,1,0:T(8,128)S(1)}, f32[1,64,512]{2,1,0:T(8,128)}, u32[]{:S(2)}) %copy-start.3) | copy-done | bytes 131096
  5.5 37.7 %outer_step_and_keys.1 = (bf16[512,512]{1,0:T(8,128)(2,1)S(1)}, f32[1,64,512]{2,1,0:T(8,128)S(1)}, f32[1,64,512]{2,1,0:T(8,128)S(1)}, bf16[4,2,2,64,512]{4,3,2,1,0:T(8,128)(2,1)S(1)}) custom-call(bf16[256,8192]{1,0:T(8,128)(2,1)} %tokens.1, bf16[1,8192]{1,0:T(2,128)(2,1)S(1)} %reshape.17.gain, bf16[1,8192,512]{2,1,0:T(8,128)(2,1)} %weight.1, ...), custom_call_target="tpu_custom_call" | custom-call | tf_op jit(solution)/shard_map/outer_step_and_keys/pallas_call | solution.py:347
  43.1 0.8 %copy.15 = bf16[512,512]{1,0:T(8,128)(2,1)} copy(bf16[512,512]{1,0:T(8,128)(2,1)S(1)} %get-tuple-element.16) | data formatting | bytes 1048576
  43.9 0.7 %copy.16 = f32[1,64,512]{2,1,0:T(8,128)} copy(f32[1,64,512]{2,1,0:T(8,128)S(1)} %get-tuple-element.17) | data formatting | bytes 262144
  44.6 0.7 %copy.17 = f32[1,64,512]{2,1,0:T(8,128)} copy(f32[1,64,512]{2,1,0:T(8,128)S(1)} %get-tuple-element.18) | data formatting | bytes 262144
  45.3 1.0 %copy.18 = bf16[1,1024,512]{2,1,0:T(8,128)(2,1)} copy(bf16[1,1024,512]{2,1,0:T(8,128)(2,1)S(1)} %bitcast.3) | data formatting | bytes 2097152
Async XLA Ops:
  1.4 1.2 %copy-start = (bf16[1,1,1024,512]{3,2,1,0:T(8,128)(2,1)S(1)}, bf16[1,1,1024,512]{3,2,1,0:T(8,128)(2,1)}, u32[]{:S(2)}) copy-start(bf16[1,1,1024,512]{3,2,1,0:T(8,128)(2,1)} %param.10) | copy-start | bytes 3145732
  2.6 1.0 %copy-start.1 = (f32[2,512,128]{2,1,0:T(8,128)S(1)}, f32[2,512,128]{2,1,0:T(8,128)}, u32[]{:S(2)}) copy-start(f32[2,512,128]{2,1,0:T(8,128)} %constant.2.clone.tables) | copy-start | bytes 1572868
  3.6 0.9 %copy-start.2 = (f32[1,64,512]{2,1,0:T(8,128)S(1)}, f32[1,64,512]{2,1,0:T(8,128)}, u32[]{:S(2)}) copy-start(f32[1,64,512]{2,1,0:T(8,128)} %outer.1) | copy-start | bytes 393220
  4.5 0.9 %copy-start.3 = (f32[1,64,512]{2,1,0:T(8,128)S(1)}, f32[1,64,512]{2,1,0:T(8,128)}, u32[]{:S(2)}) copy-start(f32[1,64,512]{2,1,0:T(8,128)} %moment.1) | copy-start | bytes 393220

commit v2 on v1

--- a/solution.py
+++ b/solution.py
@@ -22,6 +22,7 @@
 NORM_ROWS = 32
 NORM_COLS = 512
 K_STEP = 1024
+VMEM_GRANT = 64 * 2**20 - 2**16
 
 
 def rotary_tables(rows):
@@ -40,14 +41,13 @@
     tokens, gain, weight, inner, outer, moment, tables,
     keys_out, outer_out, moment_out, synced,
     tok_v, gain_v, w_v, inner_v, outer_v, moment_v, tables_v, normed_v, acc_v, keys_v,
-    rs1a, rs1b, part1a, part1b, keepa, keepb, rs2a, rs2b, part2, own, rs3, piece_v,
+    rs1, part1, keep, rs2, part2, own, rs3, piece_v,
     load_sem, tok_sem, w_sem, store_sem,
     s1_send, s1_recv, s2_send, s2_recv, s3_send, s3_recv,
-    gz_send, gz_recv, gx_send, gx_recv, gy_send, gy_recv, dx_send, dx_recv, dy_send, dy_recv,
+    gz_send, gz_recv, gx_send, gx_recv, gy_send, gy_recv, diag_send, diag_recv,
     n_send, n_recv,
 ):
     Z, T, tr, D, nc, rp, FC, nch, nw = sizes
-    H = FC // 2
     R = Z * 4
     rep = lax.axis_index("replica")
     me_t = lax.axis_index("tensor")
@@ -117,15 +117,13 @@
         sent.append(copy)
         return copy
 
-    first_a, first_b = [], []
+    by_x = [o % 2 == 0 for o in offsets]
+    first = []
     for d, o in enumerate(offsets):
         zc = z_at(o)
-        first_a.append(start(remote(
-            inner.at[zc, :, ox, :, pl.ds(0, H)], rs1a.at[d],
-            s1_send.at[2 * d], s1_recv.at[2 * d], x_peer)))
-        first_b.append(start(remote(
-            inner.at[zc, oy, :, :, pl.ds(H, H)], rs1b.at[d],
-            s1_send.at[2 * d + 1], s1_recv.at[2 * d + 1], y_peer)))
+        src = inner.at[zc, :, ox] if by_x[d] else inner.at[zc, oy]
+        first.append(start(remote(
+            src, rs1.at[d], s1_send.at[d], s1_recv.at[d], x_peer if by_x[d] else y_peer)))
 
     def norm_copy(k, c, source, device):
         rows = pl.ds(c * rows_per, rows_per)
@@ -149,41 +147,35 @@
             for j in range(0, D, NORM_COLS):
                 cols = pl.ds(j, NORM_COLS)
                 v = tok_v[rows, cols].astype(F32)
-                normed_v[me_t, rows, cols] = (v * scale * gain_v[:, cols].astype(F32)).astype(BF16)
+                normed_v[me_t, rows, cols] = (v * scale * gain_v[cols].astype(F32).reshape(1, NORM_COLS)).astype(BF16)
             return carry
 
         lax.fori_loop(0, rows_per // NORM_ROWS, block, 0)
         for k in range(1, T):
             start(norm_copy(k, c, me_t, (rep, lax.rem(me_t + k, T))))
 
-    second_a, second_b, third = [None] * Z, [None] * Z, [None] * Z
+    second, third = [None] * Z, [None] * Z
 
     def step_a(d):
         zc = z_at(offsets[d])
         if d == 0:
             load_inner.wait()
-        first_a[d].wait_recv()
-        part1a[d] = (inner_v[zc, oy, x, :, :H].astype(F32) + rs1a[d, oy].astype(F32)).astype(BF16)
-        second_a[d] = start(remote(
-            part1a.at[d], rs2a.at[d], s2_send.at[2 * d], s2_recv.at[2 * d], y_peer))
-        keepa[d] = inner_v[zc, y, x, :, :H].astype(F32) + rs1a[d, y].astype(F32)
-        first_b[d].wait_recv()
-        part1b[d] = (inner_v[zc, y, ox, :, H:].astype(F32) + rs1b[d, ox].astype(F32)).astype(BF16)
-        second_b[d] = start(remote(
-            part1b.at[d], rs2b.at[d], s2_send.at[2 * d + 1], s2_recv.at[2 * d + 1], x_peer))
-        keepb[d] = inner_v[zc, y, x, :, H:].astype(F32) + rs1b[d, x].astype(F32)
+        first[d].wait_recv()
+        if by_x[d]:
+            mine, other, to, peer = y, inner_v[zc, oy, x], oy, y_peer
+        else:
+            mine, other, to, peer = x, inner_v[zc, y, ox], ox, x_peer
+        part1[d] = (other.astype(F32) + rs1[d, to].astype(F32)).astype(BF16)
+        second[d] = start(remote(part1.at[d], rs2.at[d], s2_send.at[d], s2_recv.at[d], peer))
+        keep[d] = inner_v[zc, y, x].astype(F32) + rs1[d, mine].astype(F32)
 
     def step_b(d):
-        second_a[d].wait_recv()
-        second_b[d].wait_recv()
-        suma = keepa[d] + rs2a[d].astype(F32)
-        sumb = keepb[d] + rs2b[d].astype(F32)
+        second[d].wait_recv()
+        total = keep[d] + rs2[d].astype(F32)
         if d == last:
-            own[:, :H] = suma
-            own[:, H:] = sumb
+            own[...] = total
         else:
-            part2[d, :, :H] = suma.astype(BF16)
-            part2[d, :, H:] = sumb.astype(BF16)
+            part2[d] = total.astype(BF16)
             third[d] = start(remote(
                 part2.at[d], rs3.at[d], s3_send.at[d], s3_recv.at[d], z_peer(offsets[d])))
 
@@ -195,7 +187,7 @@
         stores.append(copy)
 
     here = synced.at[z, y, x]
-    gather_z, gather_x, gather_y, diag_x, diag_y = ([None] * Z for _ in range(5))
+    gather_z, gather_x, gather_y, diag = ([None] * Z for _ in range(4))
 
     def spread(d, src):
         zp = lax.rem(z + Z - offsets[d], Z)
@@ -232,12 +224,13 @@
 
     def step_f(d):
         zp = lax.rem(z + Z - offsets[d], Z)
-        gather_y[d].wait_recv()
-        from_y = synced.at[zp, oy, x, :, pl.ds(0, H)]
-        diag_x[d] = start(remote(from_y, from_y, dx_send.at[d], dx_recv.at[d], x_peer))
-        gather_x[d].wait_recv()
-        from_x = synced.at[zp, y, ox, :, pl.ds(H, H)]
-        diag_y[d] = start(remote(from_x, from_x, dy_send.at[d], dy_recv.at[d], y_peer))
+        if by_x[d]:
+            gather_y[d].wait_recv()
+            piece, peer = synced.at[zp, oy, x], x_peer
+        else:
+            gather_x[d].wait_recv()
+            piece, peer = synced.at[zp, y, ox], y_peer
+        diag[d] = start(remote(piece, piece, diag_send.at[d], diag_recv.at[d], peer))
 
     def project(k, part):
         slot = lax.rem(me_t + T - k, T)
@@ -288,25 +281,31 @@
         step_a(d)
         if d >= 1:
             step_b(d - 1)
-    work(1)
     step_b(last)
-    work(max(3, len(compute) - 5))
+    work(nw + 1 - max(0, Z - nch) - (1 if Z < nch else 0))
     step_c()
-    work(1)
     step_f(last)
     for d in range(last):
+        step_z(d)
         work(1)
-        step_z(d)
-        if d >= 1:
-            step_f(d - 1)
+        step_f(d)
+        work(1)
     work(len(compute))
-    step_f(last - 1)
     for d in range(Z):
-        diag_x[d].wait_recv()
-        diag_y[d].wait_recv()
+        (gather_x if by_x[d] else gather_y)[d].wait_recv()
+        diag[d].wait_recv()
     for copy in sent:
         copy.wait_send()
     for copy in stores:
+        copy.wait()
+
+
+def write_out(keys, outer, moment, synced, keys_out, outer_out, moment_out, synced_out, sem):
+    pairs = ((synced, synced_out), (keys, keys_out), (outer, outer_out), (moment, moment_out))
+    copies = [pltpu.make_async_copy(a, b, sem.at[i]) for i, (a, b) in enumerate(pairs)]
+    for copy in copies:
+        copy.start()
+    for copy in copies:
         copy.wait()
 
 
@@ -319,28 +318,24 @@
         nc = key_weight.shape[2]
         rows, FC = inner_params.shape[2:]
         rp = rows // R
-        H = FC // 2
         tok = tr * T
         nch = max(1, tr // 64)
         nw = 4
         inner = inner_params.reshape(Z, 2, 2, rp, FC)
-        gain = norm_gain.reshape(1, D)
         tables = jnp.asarray(rotary_tables(tok))
         sizes = (Z, T, tr, D, nc, rp, FC, nch, nw)
         vm = pltpu.VMEM
         dma = lambda n: pltpu.SemaphoreType.DMA((n,))
         scratch = [
-            vm((tr, D), BF16), vm((1, D), BF16), vm((D, nc), BF16),
+            vm((tr, D), BF16), vm((D,), BF16), vm((D, nc), BF16),
             vm((Z, 2, 2, rp, FC), BF16), vm((1, rp, FC), F32), vm((1, rp, FC), F32),
             vm((2, tok, HD), F32), vm((T, tr, D), BF16), vm((tr, nc), F32), vm((tok, nc), BF16),
-            vm((Z, 2, rp, H), BF16), vm((Z, 2, rp, H), BF16),
-            vm((Z, rp, H), BF16), vm((Z, rp, H), BF16),
-            vm((Z, rp, H), F32), vm((Z, rp, H), F32),
-            vm((Z, rp, H), BF16), vm((Z, rp, H), BF16),
-            vm((Z, rp, FC), BF16), vm((rp, FC), F32), vm((Z, rp, FC), BF16), vm((rp, FC), BF16),
+            vm((Z, 2, rp, FC), BF16), vm((Z, rp, FC), BF16), vm((Z, rp, FC), F32),
+            vm((Z, rp, FC), BF16), vm((Z, rp, FC), BF16), vm((rp, FC), F32),
+            vm((Z, rp, FC), BF16), vm((rp, FC), BF16),
             dma(5), dma(nch), dma(nw), dma(3 + T),
-            dma(2 * Z), dma(2 * Z), dma(2 * Z), dma(2 * Z), dma(Z), dma(Z),
-            dma(Z), dma(Z), dma(Z), dma(Z), dma(Z), dma(Z), dma(Z), dma(Z), dma(Z), dma(Z),
+            dma(Z), dma(Z), dma(Z), dma(Z), dma(Z), dma(Z),
+            dma(Z), dma(Z), dma(Z), dma(Z), dma(Z), dma(Z), dma(Z), dma(Z),
             dma(nch * (T - 1)), dma(nch * (T - 1)),
         ]
         anywhere = pl.BlockSpec(memory_space=pl.ANY)
@@ -356,11 +351,24 @@
             out_specs=(anywhere,) * 4,
             scratch_shapes=scratch,
             compiler_params=pltpu.CompilerParams(
-                collective_id=0, has_side_effects=True, vmem_limit_bytes=48 * 2**20
+                collective_id=0, has_side_effects=True, vmem_limit_bytes=VMEM_GRANT
             ),
             name="outer_step_and_keys",
-        )(tokens, gain, key_weight, inner, outer_params, outer_momentum, tables)
-        return keys, outer_next, moment_next, synced.reshape(1, rows, FC)
+        )(tokens, norm_gain, key_weight, inner, outer_params, outer_momentum, tables)
+        return pl.pallas_call(
+            write_out,
+            out_shape=(
+                jax.ShapeDtypeStruct((tok, nc), BF16),
+                jax.ShapeDtypeStruct((1, rp, FC), F32),
+                jax.ShapeDtypeStruct((1, rp, FC), F32),
+                jax.ShapeDtypeStruct((1, rows, FC), BF16),
+            ),
+            in_specs=[anywhere] * 4,
+            out_specs=(pl.BlockSpec(memory_space=pltpu.HBM),) * 4,
+            scratch_shapes=[dma(4)],
+            compiler_params=pltpu.CompilerParams(vmem_limit_bytes=VMEM_GRANT),
+            name="write_out",
+        )(keys, outer_next, moment_next, synced.reshape(1, rows, FC))
 
     in_specs = (
         P(("replica", "tensor"), None),

time: 46.5 us -> 102 us (2.19)
  Pallas kernels: 37.7 us -> 101 us
  local copies, waits for them, and re-layouts: 7.88 us -> 0 us
    pallas_call x0 -> x1, Pallas kernels: none -> 56.7 us  [body(): pl.pallas_call(write_out, out_shape=(jax.ShapeDtypeStruct((tok, nc), BF16...]
    unnamed x12 -> x0, local copies, waits for them, and re-layouts: 7.14 us -> none
    pallas_call x1, Pallas kernels: 37.7 us -> 44.6 us  [body(): pl.pallas_call(functools.partial(kernel, sizes), out_shape=(jax.ShapeDtyp...]
where the time goes in v2:
time: 102 us
  Pallas kernels  101 us (99%)
    pallas_call x1, Pallas kernels, body(): pl.pallas_call(write_out, out_shape=(jax.ShapeDtypeStruct((tok, nc), BF16...  56.7 us
    pallas_call x1, Pallas kernels, body(): pl.pallas_call(functools.partial(kernel, sizes), out_shape=(jax.ShapeDtyp...  44.6 us

profile of v2, /device:TPU:0, one launch (start us, length us, event | category | flops | bytes accessed | tf_op | source)
XLA Modules:
  0.0 101.9 jit_solution(4061739905956756111)
XLA Ops:
  0.6 44.6 %outer_step_and_keys.1 = (bf16[512,512]{1,0:T(8,128)(2,1)}, f32[1,64,512]{2,1,0:T(8,128)}, f32[1,64,512]{2,1,0:T(8,128)}, bf16[4,2,2,64,512]{4,3,2,1,0:T(8,128)(2,1)}) custom-call(bf16[256,8192]{1,0:T(8,128)(2,1)} %tokens.1, bf16[8192]{0:T(1024)(128)(2,1)} %gain.1, bf16[1,8192,512]{2,1,0:T(8,128)(2,1)} %weight.1, bf16[4,2,2,64,512]{4,3,2,1,0:T(8,128)(2,1)} %bitcast.3, ...), custom_call_target="tpu_custom_call" | custom-call | tf_op jit(solution)/shard_map/outer_step_and_keys/pallas_call | solution.py:342
  45.2 56.7 %write_out.1 = (bf16[512,512]{1,0:T(8,128)(2,1)}, f32[1,64,512]{2,1,0:T(8,128)}, f32[1,64,512]{2,1,0:T(8,128)}, bf16[1,1024,512]{2,1,0:T(8,128)(2,1)}) custom-call(bf16[512,512]{1,0:T(8,128)(2,1)} %get-tuple-element.8.keys, f32[1,64,512]{2,1,0:T(8,128)} %get-tuple-element.9.outer, f32[1,64,512]{2,1,0:T(8,128)} %get-tuple-element.10.moment, ...), custom_call_target="tpu_custom_call" | custom-call | tf_op jit(solution)/shard_map/write_out/pallas_call | solution.py:358

commit v3 on v2

--- a/solution.py
+++ b/solution.py
@@ -22,7 +22,7 @@
 NORM_ROWS = 32
 NORM_COLS = 512
 K_STEP = 1024
-VMEM_GRANT = 64 * 2**20 - 2**16
+VMEM_GRANT = 48 * 2**20
 
 
 def rotary_tables(rows):
@@ -85,9 +85,9 @@
         )
         for c in range(nw)
     ]
+    load_inner.start()
     load_gain.start()
     load_tok[0].start()
-    load_inner.start()
     for c in range(1, nch):
         load_tok[c].start()
     for c in range(nw):
@@ -119,9 +119,10 @@
 
     by_x = [o % 2 == 0 for o in offsets]
     first = []
+    load_inner.wait()
     for d, o in enumerate(offsets):
         zc = z_at(o)
-        src = inner.at[zc, :, ox] if by_x[d] else inner.at[zc, oy]
+        src = inner_v.at[zc, :, ox] if by_x[d] else inner_v.at[zc, oy]
         first.append(start(remote(
             src, rs1.at[d], s1_send.at[d], s1_recv.at[d], x_peer if by_x[d] else y_peer)))
 
@@ -158,8 +159,6 @@
 
     def step_a(d):
         zc = z_at(offsets[d])
-        if d == 0:
-            load_inner.wait()
         first[d].wait_recv()
         if by_x[d]:
             mine, other, to, peer = y, inner_v[zc, oy, x], oy, y_peer
@@ -338,14 +337,18 @@
             dma(Z), dma(Z), dma(Z), dma(Z), dma(Z), dma(Z), dma(Z), dma(Z),
             dma(nch * (T - 1)), dma(nch * (T - 1)),
         ]
+        operands = [
+            pltpu.with_memory_space_constraint(a, pltpu.HBM)
+            for a in (tokens, norm_gain, key_weight, inner, outer_params, outer_momentum, tables)
+        ]
         anywhere = pl.BlockSpec(memory_space=pl.ANY)
         keys, outer_next, moment_next, synced = pl.pallas_call(
             functools.partial(kernel, sizes),
             out_shape=(
-                jax.ShapeDtypeStruct((tok, nc), BF16),
-                jax.ShapeDtypeStruct((1, rp, FC), F32),
-                jax.ShapeDtypeStruct((1, rp, FC), F32),
-                jax.ShapeDtypeStruct((Z, 2, 2, rp, FC), BF16),
+                vm((tok, nc), BF16),
+                vm((1, rp, FC), F32),
+                vm((1, rp, FC), F32),
+                vm((Z, 2, 2, rp, FC), BF16),
             ),
             in_specs=[anywhere] * 7,
             out_specs=(anywhere,) * 4,
@@ -354,7 +357,7 @@
                 collective_id=0, has_side_effects=True, vmem_limit_bytes=VMEM_GRANT
             ),
             name="outer_step_and_keys",
-        )(tokens, norm_gain, key_weight, inner, outer_params, outer_momentum, tables)
+        )(*operands)
         return pl.pallas_call(
             write_out,
             out_shape=(
@@ -366,7 +369,6 @@
             in_specs=[anywhere] * 4,
             out_specs=(pl.BlockSpec(memory_space=pltpu.HBM),) * 4,
             scratch_shapes=[dma(4)],
-            compiler_params=pltpu.CompilerParams(vmem_limit_bytes=VMEM_GRANT),
             name="write_out",
         )(keys, outer_next, moment_next, synced.reshape(1, rows, FC))
 

time: 102 us -> 103 us (level)
  local copies, waits for them, and re-layouts: 0 us -> 3.06 us
  Pallas kernels: 101 us -> 99.1 us
    unnamed x0 -> x8, local copies, waits for them, and re-layouts: none -> 3.06 us
    pallas_call x1, Pallas kernels: 44.6 us -> 42.4 us  [body(): pl.pallas_call(functools.partial(kernel, sizes), out_shape=(vm((tok, nc),...]
where the time goes in v3:
time: 103 us
  Pallas kernels  99.1 us (96%)
  local copies, waits for them, and re-layouts  3.06 us (3%)
    pallas_call x1, Pallas kernels, body(): pl.pallas_call(write_out, out_shape=(jax.ShapeDtypeStruct((tok, nc), BF16...  56.7 us
    pallas_call x1, Pallas kernels, body(): pl.pallas_call(functools.partial(kernel, sizes), out_shape=(vm((tok, nc),...  42.4 us
    unnamed x8, local copies, waits for them, and re-layouts  3.06 us

profile of v3, /device:TPU:0, one launch (start us, length us, event | category | flops | bytes accessed | tf_op | source)
XLA Modules:
  0.0 102.8 jit_solution(13809523697520195277)
XLA Ops:
  0.6 42.4 %outer_step_and_keys.1 = (bf16[512,512]{1,0:T(8,128)(2,1)S(1)}, f32[1,64,512]{2,1,0:T(8,128)S(1)}, f32[1,64,512]{2,1,0:T(8,128)S(1)}, bf16[4,2,2,64,512]{4,3,2,1,0:T(8,128)(2,1)S(1)}) custom-call(bf16[256,8192]{1,0:T(8,128)(2,1)} %tokens.1, bf16[8192]{0:T(1024)(128)(2,1)} %gain.1, bf16[1,8192,512]{2,1,0:T(8,128)(2,1)} %weight.1, ...), custom_call_target="tpu_custom_call" | custom-call | tf_op jit(solution)/shard_map/outer_step_and_keys/pallas_call | solution.py:345
  43.0 0.0 copy-start
  43.0 1.0 copy-done
  44.0 0.0 copy-start.1
  44.0 0.8 copy-done.1
  44.8 0.0 copy-start.2
  44.8 0.7 copy-done.2
  45.4 0.0 copy-start.3
  45.4 0.6 copy-done.3
  46.1 56.7 %write_out.1 = (bf16[512,512]{1,0:T(8,128)(2,1)}, f32[1,64,512]{2,1,0:T(8,128)}, f32[1,64,512]{2,1,0:T(8,128)}, bf16[1,1024,512]{2,1,0:T(8,128)(2,1)}) custom-call(bf16[512,512]{1,0:T(8,128)(2,1)} %copy-done.1, f32[1,64,512]{2,1,0:T(8,128)} %copy-done.2, f32[1,64,512]{2,1,0:T(8,128)} %copy-done.3, bf16[1,1024,512]{2,1,0:T(8,128)(2,1)} %bitcast.2), custom_call_target="tpu_custom_call" | custom-call | tf_op jit(solution)/shard_map/write_out/pallas_call | solution.py:361
Async XLA Ops:
  43.0 1.0 copy-start
  44.0 0.8 copy-start.1
  44.8 0.7 copy-start.2
  45.4 0.6 copy-start.3

commit v4 on v3

--- a/solution.py
+++ b/solution.py
@@ -40,7 +40,7 @@
     sizes,
     tokens, gain, weight, inner, outer, moment, tables,
     keys_out, outer_out, moment_out, synced,
-    tok_v, gain_v, w_v, inner_v, outer_v, moment_v, tables_v, normed_v, acc_v, keys_v,
+    tok_v, gain_v, gain_f, w_v, inner_v, outer_v, moment_v, tables_v, normed_v, acc_v, keys_v,
     rs1, part1, keep, rs2, part2, own, rs3, piece_v,
     load_sem, tok_sem, w_sem, store_sem,
     s1_send, s1_recv, s2_send, s2_recv, s3_send, s3_recv,
@@ -136,6 +136,9 @@
     def norm(c):
         if c == 0:
             load_gain.wait()
+            for j in range(0, D, NORM_COLS):
+                cols = pl.ds(j, NORM_COLS)
+                gain_f[:, cols] = gain_v[cols].astype(F32).reshape(1, NORM_COLS)
         load_tok[c].wait()
 
         def block(i, carry):
@@ -148,10 +151,12 @@
             for j in range(0, D, NORM_COLS):
                 cols = pl.ds(j, NORM_COLS)
                 v = tok_v[rows, cols].astype(F32)
-                normed_v[me_t, rows, cols] = (v * scale * gain_v[cols].astype(F32).reshape(1, NORM_COLS)).astype(BF16)
+                normed_v[me_t, rows, cols] = (v * scale * gain_f[:, cols]).astype(BF16)
             return carry
 
         lax.fori_loop(0, rows_per // NORM_ROWS, block, 0)
+
+    def send_norm(c):
         for k in range(1, T):
             start(norm_copy(k, c, me_t, (rep, lax.rem(me_t + k, T))))
 
@@ -280,7 +285,11 @@
         step_a(d)
         if d >= 1:
             step_b(d - 1)
+            if d - 1 < nch:
+                send_norm(d - 1)
     step_b(last)
+    for c in range(last, nch):
+        send_norm(c)
     work(nw + 1 - max(0, Z - nch) - (1 if Z < nch else 0))
     step_c()
     step_f(last)
@@ -326,7 +335,7 @@
         vm = pltpu.VMEM
         dma = lambda n: pltpu.SemaphoreType.DMA((n,))
         scratch = [
-            vm((tr, D), BF16), vm((D,), BF16), vm((D, nc), BF16),
+            vm((tr, D), BF16), vm((D,), BF16), vm((1, D), F32), vm((D, nc), BF16),
             vm((Z, 2, 2, rp, FC), BF16), vm((1, rp, FC), F32), vm((1, rp, FC), F32),
             vm((2, tok, HD), F32), vm((T, tr, D), BF16), vm((tr, nc), F32), vm((tok, nc), BF16),
             vm((Z, 2, rp, FC), BF16), vm((Z, rp, FC), BF16), vm((Z, rp, FC), F32),
@@ -358,6 +367,10 @@
             ),
             name="outer_step_and_keys",
         )(*operands)
+        results = [
+            pltpu.with_memory_space_constraint(a, pltpu.VMEM)
+            for a in (keys, outer_next, moment_next, synced.reshape(1, rows, FC))
+        ]
         return pl.pallas_call(
             write_out,
             out_shape=(
@@ -369,8 +382,9 @@
             in_specs=[anywhere] * 4,
             out_specs=(pl.BlockSpec(memory_space=pltpu.HBM),) * 4,
             scratch_shapes=[dma(4)],
+            compiler_params=pltpu.CompilerParams(vmem_limit_bytes=16 * 2**20),
             name="write_out",
-        )(keys, outer_next, moment_next, synced.reshape(1, rows, FC))
+        )(*results)
 
     in_specs = (
         P(("replica", "tensor"), None),

time: 103 us -> 46.8 us (0.45)
  Pallas kernels: 99.1 us -> 46 us
  local copies, waits for them, and re-layouts: 3.06 us -> 0 us
    pallas_call x1, Pallas kernels: 56.7 us -> 1.25 us  [body(): pl.pallas_call(write_out, out_shape=(jax.ShapeDtypeStruct((tok, nc), BF16...]
    unnamed x8 -> x0, local copies, waits for them, and re-layouts: 3.06 us -> none
    pallas_call x1, Pallas kernels: 42.4 us -> 44.8 us  [body(): pl.pallas_call(functools.partial(kernel, sizes), out_shape=(vm((tok, nc),...]
where the time goes in v4:
time: 46.8 us; the launch traced here: 46.7 us
  Pallas kernels  46 us (98%)
  between operations  0.64 us (1%)
    pallas_call x1, Pallas kernels, body(): pl.pallas_call(functools.partial(kernel, sizes), out_shape=(vm((tok, nc),...  44.8 us
    pallas_call x1, Pallas kernels, body(): pl.pallas_call(write_out, out_shape=(jax.ShapeDtypeStruct((tok, nc), BF16...  1.25 us

profile of v4, /device:TPU:0, one launch (start us, length us, event | category | flops | bytes accessed | tf_op | source)
XLA Modules:
  0.0 46.7 jit_solution(4799192200605499280)
XLA Ops:
  0.6 44.8 %outer_step_and_keys.1 = (bf16[512,512]{1,0:T(8,128)(2,1)S(1)}, f32[1,64,512]{2,1,0:T(8,128)S(1)}, f32[1,64,512]{2,1,0:T(8,128)S(1)}, bf16[4,2,2,64,512]{4,3,2,1,0:T(8,128)(2,1)S(1)}) custom-call(bf16[256,8192]{1,0:T(8,128)(2,1)} %tokens.1, bf16[8192]{0:T(1024)(128)(2,1)} %gain.1, bf16[1,8192,512]{2,1,0:T(8,128)(2,1)} %weight.1, ...), custom_call_target="tpu_custom_call" | custom-call | tf_op jit(solution)/shard_map/outer_step_and_keys/pallas_call | solution.py:354
  45.4 1.3 %write_out.1 = (bf16[512,512]{1,0:T(8,128)(2,1)}, f32[1,64,512]{2,1,0:T(8,128)}, f32[1,64,512]{2,1,0:T(8,128)}, bf16[1,1024,512]{2,1,0:T(8,128)(2,1)}) custom-call(bf16[512,512]{1,0:T(8,128)(2,1)S(1)} %get-tuple-element.8.keys, f32[1,64,512]{2,1,0:T(8,128)S(1)} %get-tuple-element.9.outer, f32[1,64,512]{2,1,0:T(8,128)S(1)} %get-tuple-element.10.moment, ...), custom_call_target="tpu_custom_call" | custom-call | tf_op jit(solution)/shard_map/write_out/pallas_call | solution.py:374

commit v5 on v4

--- a/solution.py
+++ b/solution.py
@@ -155,8 +155,6 @@
             return carry
 
         lax.fori_loop(0, rows_per // NORM_ROWS, block, 0)
-
-    def send_norm(c):
         for k in range(1, T):
             start(norm_copy(k, c, me_t, (rep, lax.rem(me_t + k, T))))
 
@@ -285,19 +283,15 @@
         step_a(d)
         if d >= 1:
             step_b(d - 1)
-            if d - 1 < nch:
-                send_norm(d - 1)
     step_b(last)
-    for c in range(last, nch):
-        send_norm(c)
-    work(nw + 1 - max(0, Z - nch) - (1 if Z < nch else 0))
+    work(len(compute) - (T - 1) * (nw + 1))
     step_c()
     step_f(last)
     for d in range(last):
         step_z(d)
-        work(1)
         step_f(d)
-        work(1)
+        if d == last - 2:
+            work(2)
     work(len(compute))
     for d in range(Z):
         (gather_x if by_x[d] else gather_y)[d].wait_recv()

time: 46.8 us -> 44.1 us (0.942)
  Pallas kernels: 46 us -> 43.3 us
    pallas_call x1, Pallas kernels: 44.8 us -> 42 us  [body(): pl.pallas_call(functools.partial(kernel, sizes), out_shape=(vm((tok, nc),...]
where the time goes in v5:
time: 44.1 us; the launch traced here: 43.9 us
  Pallas kernels  43.3 us (98%)
  between operations  0.64 us (1%)
    pallas_call x1, Pallas kernels, body(): pl.pallas_call(functools.partial(kernel, sizes), out_shape=(vm((tok, nc),...  42 us
    pallas_call x1, Pallas kernels, body(): pl.pallas_call(write_out, out_shape=(jax.ShapeDtypeStruct((tok, nc), BF16...  1.25 us

profile of v5, /device:TPU:0, one launch (start us, length us, event | category | flops | bytes accessed | tf_op | source)
XLA Modules:
  0.0 43.9 jit_solution(17837014133977838332)
XLA Ops:
  0.6 42.0 %outer_step_and_keys.1 = (bf16[512,512]{1,0:T(8,128)(2,1)S(1)}, f32[1,64,512]{2,1,0:T(8,128)S(1)}, f32[1,64,512]{2,1,0:T(8,128)S(1)}, bf16[4,2,2,64,512]{4,3,2,1,0:T(8,128)(2,1)S(1)}) custom-call(bf16[256,8192]{1,0:T(8,128)(2,1)} %tokens.1, bf16[8192]{0:T(1024)(128)(2,1)} %gain.1, bf16[1,8192,512]{2,1,0:T(8,128)(2,1)} %weight.1, ...), custom_call_target="tpu_custom_call" | custom-call | tf_op jit(solution)/shard_map/outer_step_and_keys/pallas_call | solution.py:348
  42.7 1.3 %write_out.1 = (bf16[512,512]{1,0:T(8,128)(2,1)}, f32[1,64,512]{2,1,0:T(8,128)}, f32[1,64,512]{2,1,0:T(8,128)}, bf16[1,1024,512]{2,1,0:T(8,128)(2,1)}) custom-call(bf16[512,512]{1,0:T(8,128)(2,1)S(1)} %get-tuple-element.8.keys, f32[1,64,512]{2,1,0:T(8,128)S(1)} %get-tuple-element.9.outer, f32[1,64,512]{2,1,0:T(8,128)S(1)} %get-tuple-element.10.moment, ...), custom_call_target="tpu_custom_call" | custom-call | tf_op jit(solution)/shard_map/write_out/pallas_call | solution.py:368

commit v6 on v5

--- a/solution.py
+++ b/solution.py
@@ -277,7 +277,7 @@
             if compute:
                 compute.pop()()
 
-    work(1)
+    work(nch)
     for d in range(Z):
         work(1)
         step_a(d)

time: 44.1 us -> 44.4 us (level)
  no operation moved by 1% of the time
where the time goes in v6:
time: 44.4 us; the launch traced here: 44.2 us
  Pallas kernels  43.6 us (98%)
  between operations  0.64 us (1%)
    pallas_call x1, Pallas kernels, body(): pl.pallas_call(functools.partial(kernel, sizes), out_shape=(vm((tok, nc),...  42.3 us
    pallas_call x1, Pallas kernels, body(): pl.pallas_call(write_out, out_shape=(jax.ShapeDtypeStruct((tok, nc), BF16...  1.25 us

profile of v6, /device:TPU:0, one launch (start us, length us, event | category | flops | bytes accessed | tf_op | source)
XLA Modules:
  0.0 44.2 jit_solution(11765590219756745525)
XLA Ops:
  0.6 42.3 %outer_step_and_keys.1 = (bf16[512,512]{1,0:T(8,128)(2,1)S(1)}, f32[1,64,512]{2,1,0:T(8,128)S(1)}, f32[1,64,512]{2,1,0:T(8,128)S(1)}, bf16[4,2,2,64,512]{4,3,2,1,0:T(8,128)(2,1)S(1)}) custom-call(bf16[256,8192]{1,0:T(8,128)(2,1)} %tokens.1, bf16[8192]{0:T(1024)(128)(2,1)} %gain.1, bf16[1,8192,512]{2,1,0:T(8,128)(2,1)} %weight.1, ...), custom_call_target="tpu_custom_call" | custom-call | tf_op jit(solution)/shard_map/outer_step_and_keys/pallas_call | solution.py:348
  43.0 1.3 %write_out.1 = (bf16[512,512]{1,0:T(8,128)(2,1)}, f32[1,64,512]{2,1,0:T(8,128)}, f32[1,64,512]{2,1,0:T(8,128)}, bf16[1,1024,512]{2,1,0:T(8,128)(2,1)}) custom-call(bf16[512,512]{1,0:T(8,128)(2,1)S(1)} %get-tuple-element.8.keys, f32[1,64,512]{2,1,0:T(8,128)S(1)} %get-tuple-element.9.outer, f32[1,64,512]{2,1,0:T(8,128)S(1)} %get-tuple-element.10.moment, ...), custom_call_target="tpu_custom_call" | custom-call | tf_op jit(solution)/shard_map/write_out/pallas_call | solution.py:368
